TPU v7x, 512 devices: a whole 4x4x16 slice. The times are simulated.
512 devices in a mesh: row: 32 (over x, y, core), col: 16 (over z).
Axes of the slice: x: 4, y: 4, z: 16, core: 2. Of those that a mesh axis runs over, the one named last changes fastest.
Arguments:
- z_anc: float32 [8192, 8192], P('row', 'col'), may hold values from -0.5 to 0.5
- in_one: int32 [64], replicated, may hold values from 0 to 1
- in_two: int32 [64], replicated, may hold values from 0 to 1, as said below
- l_one: float32 [8192, 512], P(('row', 'col')), may hold values from -0.015625 to 0.015625
- l_two: float32 [8192, 512], P(('row', 'col')), may hold values from -0.015625 to 0.015625
- l_pair: float32 [512, 512], P('row'), may hold values from -0.25 to 0.25
- linv_one: float32 [512, 512], replicated, as said below
- linv_two: float32 [512, 512], replicated, as said below
Outputs:
- col_one: float32 [8192, 512], P(('row', 'col'))
- diag_one: float32 [512, 512], P('row', 'col')
- col_two: float32 [8192, 512], P(('row', 'col'))
- pair_block: float32 [512, 512], P('row', 'col')
- diag_two: float32 [512, 512], P('row', 'col')
Inputs may be any that keep to these rules, and one draw needn't show every extreme that they name: `in_two`: a block in the second supernode's ancestor structure is also in the first supernode's structure. `linv_one`: lower triangular, diagonal between 0.5 and 1.5. `linv_two`: lower triangular, diagonal between 0.5 and 1.5.
All inputs are finite; a program needn't handle non-finite values.
Results may differ from a plain program's by a relative error of at most 0.00003.
Values sent between devices are 32-bit elements; how exact they have to be, the bound alone decides.
A program may use at most 64 MiB of HBM per device.

v0:
```python
from functools import partial

import jax
import jax.numpy as jnp
from jax import lax
from jax.sharding import PartitionSpec as P

BLK = 128


def spread_2(value, axis, source):
    kept = jnp.where(lax.axis_index(axis) == source, value, 0).astype(value.dtype)
    return lax.psum(kept, axis)


def shards(z_anc, in_one, in_two, l_one, l_two, l_pair, linv_one, linv_two):
    highest = lax.Precision.HIGHEST
    product = partial(jnp.dot, precision=highest, preferred_element_type=jnp.float32)
    row_count = lax.axis_size("row")
    col_count = lax.axis_size("col")
    ratio = row_count // col_count
    row_pos = lax.axis_index("row")
    col_pos = lax.axis_index("col")
    rows_dev = z_anc.shape[0]
    fine = l_one.shape[0]
    width = linv_one.shape[0]
    global_rows = row_pos * rows_dev + col_pos * fine + jnp.arange(fine, dtype=jnp.int32)
    table = jnp.arange(in_one.shape[0], dtype=jnp.int32)
    hits = (global_rows[:, None] // BLK == table[None, :]).astype(jnp.float32)
    mask_one = product(hits, in_one.astype(jnp.float32))[:, None]
    mask_two = product(hits, in_two.astype(jnp.float32))[:, None]
    u_one = mask_one * product(l_one, linv_one)
    u_two = mask_two * product(l_two, linv_two)
    u_pair = lax.all_gather(product(l_pair, linv_two), "row", axis=0, tiled=True)
    tile_rows = width // row_count
    tile_cols = width // col_count
    row_start = row_pos * tile_rows
    col_start = col_pos * tile_cols

    def tile(matrix):
        return lax.dynamic_slice(matrix, (row_start, col_start), (tile_rows, tile_cols))

    def ancestor_products(near_list, far_list, reducer):
        far_all = far_list[0]
        early = [None for near in near_list]

        def make_rows(start, count):
            return product(z_anc, far_all)

        summed = reducer(make_rows)
        return (jnp.split(summed, len(near_list), axis=1), early)

    def spread(u_fine):
        near = lax.all_gather(u_fine, "col", axis=0, tiled=True)
        far = jnp.concatenate(
            [
                jax.tree.map(lambda part: spread_2(part, "row", col_pos * ratio + step), near)
                for step in range(ratio)
            ],
            axis=0,
        )
        return (near, far)

    def single_reduce(make):
        return lax.psum_scatter(
            make(jnp.int32(0), rows_dev // col_count * lax.axis_size("col")),
            "col",
            scatter_dimension=0,
            tiled=True,
        )

    near_one, far_one = spread(u_one)
    results, earlies = ancestor_products([near_one], [far_one], single_reduce)
    y_one = results[0]
    early_one = earlies[0]
    col_one = -(mask_one * y_one)
    one_partial = product(u_one.T, y_one)
    gram_one = product(linv_one.T, linv_one)
    diag_one = gram_one + lax.psum(one_partial, ("row", "col"))
    near_two, far_two = spread(u_two)
    results, earlies = ancestor_products([near_two], [far_two], single_reduce)
    base_two = results[0]
    early_two = earlies[0]
    local_term = product(col_one, u_pair)
    y_two = base_two + local_term
    two_partial = product(u_two.T, y_two)
    cross_partial = product(col_one.T, u_two)
    col_two = -(mask_two * y_two)
    linv_rows = lax.dynamic_slice_in_dim(linv_two, row_start, tile_rows, 1)
    linv_cols = lax.dynamic_slice_in_dim(linv_two, col_start, tile_cols, 1)
    pair_rows_part = lax.dynamic_slice_in_dim(u_pair, row_start, tile_rows, 1)
    cross_sum, two_sum = lax.psum((cross_partial, two_partial), ("row", "col"))
    y_pair = cross_sum + product(diag_one, u_pair)
    y_pair_cols = lax.dynamic_slice_in_dim(y_pair, col_start, tile_cols, 1)
    diag_two = (
        product(linv_rows.T, linv_cols) + tile(two_sum) + product(pair_rows_part.T, y_pair_cols)
    )
    return (col_one, tile(diag_one), col_two, tile(-y_pair), diag_two)


def solution(mesh):
    placed = (
        P("row", "col"),
        P(),
        P(),
        P(("row", "col"), None),
        P(("row", "col"), None),
        P("row", None),
        P(),
        P(),
    )
    return jax.shard_map(
        shards,
        mesh=mesh,
        in_specs=placed,
        out_specs=(
            P(("row", "col"), None),
            P("row", "col"),
            P(("row", "col"), None),
            P("row", "col"),
            P("row", "col"),
        ),
        check_vma=False,
    )
```

profile of v0, /device:TPU:1, one launch (start us, length us, event | category | flops | bytes accessed | tf_op | source)
XLA Modules:
  0.0 925.5 jit_solution(18414904308156066149)
XLA Ops:
  7.3 1.0 convolution_bitcast_fusion.3
  8.2 0.9 convolution_bitcast_fusion.2
  9.1 1.4 convolution_multiply_fusion.1
  10.5 31.9 %all_gather.9 = f32[256,512]{1,0:T(8,128)S(1)} all-gather(f32[16,512]{1,0:T(8,128)S(1)} %convolution_multiply_fusion.1), channel_id=1, replica_groups=mesh['row'=32,'col'=16] {'col'}, dimensions={0}, use_global_device_ids=true | all-gather | bytes 557056 | tf_op jit(solution)/shard_map/all_gather | solution.py:54
  42.4 0.6 convolution_multiply_fusion
  43.0 23.0 %all_gather.10 = f32[256,512]{1,0:T(8,128)S(1)} all-gather(f32[16,512]{1,0:T(8,128)S(1)} %convolution_multiply_fusion), channel_id=1, replica_groups=mesh['row'=32,'col'=16] {'col'}, dimensions={0}, use_global_device_ids=true | all-gather | bytes 557056 | tf_op jit(solution)/shard_map/all_gather | solution.py:54
  66.0 1.1 broadcast_select_fusion.1
  67.2 1.1 broadcast_select_fusion.3
  68.3 0.0 reduce-scatter.3.cloned.1.call-start
  68.3 148.8 %all-reduce.7.cloned.1.call-done = (f32[256,512]{1,0:T(8,128)}, f32[256,512]{1,0:T(8,128)}, f32[256,512]{1,0:T(8,128)}, f32[256,512]{1,0:T(8,128)}) async-done(((f32[256,512]{1,0:T(8,128)}, f32[256,512]{1,0:T(8,128)}, f32[256,512]{1,0:T(8,128)}, f32[256,512]{1,0:T(8,128)}), (f32[256,512]{1,0:T(8,128)}, f32[256,512]{1,0:T(8,128)}, f32[256,512]{1,0:T(8,128)}, ...) | async-done | bytes 2097168 | tf_op jit(solution)/shard_map/psum | solution.py:13
  217.2 3.1 convolution_bitcast_fusion.1
  220.3 0.0 all-gather.2.cloned.1.call-start
  220.4 0.7 copy-done.9
  221.0 1.2 fusion.17
  222.3 0.0 reduce-scatter.5.cloned.1.call-start
  222.3 2.9 convolution_bitcast_fusion
  225.3 0.2 all-reduce.5.cloned.1.call-start
  225.5 52.6 %reduce-scatter.3.cloned.1.call-done = f32[16,512]{1,0:T(8,128)} async-done(((f32[256,512]{1,0:T(8,128)}), f32[16,512]{1,0:T(8,128)}) %reduce-scatter.3.cloned.1.call-update) | async-done | bytes 32784 | tf_op jit(solution)/shard_map/reduce_scatter | solution.py:65
  278.1 0.8 multiply_negate_fusion.1
  279.0 2.0 fusion.18
  281.0 68.8 %all-gather.2.cloned.1.call-done = f32[512,512]{1,0:T(8,128)} async-done(((f32[16,512]{1,0:T(8,128)}), f32[512,512]{1,0:T(8,128)}) %all-gather.2.cloned.1.call-update) | async-done | bytes 1048592 | tf_op jit(solution)/shard_map/all_gather | solution.py:34
  349.7 60.1 %reduce-scatter.5.cloned.1.call-done = f32[16,512]{1,0:T(8,128)} async-done(((f32[256,512]{1,0:T(8,128)}), f32[16,512]{1,0:T(8,128)}) %reduce-scatter.5.cloned.1.call-update) | async-done | bytes 32784 | tf_op jit(solution)/shard_map/reduce_scatter | solution.py:65
  409.8 2.5 multiply_negate_fusion
  412.3 2.0 fusion.19
  414.3 2.0 fusion.16
  416.3 493.4 %all-reduce.5.cloned.1.call-done = (f32[512,512]{1,0:T(8,128)}, f32[512,512]{1,0:T(8,128)}, f32[512,512]{1,0:T(8,128)}) async-done(((f32[512,512]{1,0:T(8,128)}, f32[512,512]{1,0:T(8,128)}, f32[512,512]{1,0:T(8,128)}), (f32[512,512]{1,0:T(8,128)}, f32[512,512]{1,0:T(8,128)}, f32[512,512]{1,0:T(8,128)})) %all-reduce.5.cloned.1.call-update) | async-done | bytes 3145744 | tf_op jit(solution)/shard_map/psum | solution.py:79
  909.8 3.2 convolution_add_fusion.1
  913.0 0.7 dynamic_slice.21
  913.7 1.8 convolution_add_fusion
  915.6 0.7 dynamic-slice_negate_fusion
  916.2 1.4 convolution_add_fusion.4
  917.6 1.4 convolution_add_fusion.3
  (26 shorter events, 0.2 us)
Async XLA Ops:
  7.2 1.9 copy-start
  7.2 35.2 %copy-start.1 = (f32[512,512]{1,0:T(8,128)S(1)}, f32[512,512]{1,0:T(8,128)}, u32[]{:S(2)}) copy-start(f32[512,512]{1,0:T(8,128)} %param.15) | copy-start | bytes 3145732
  7.2 210.0 %all-reduce.7.cloned.1.call-start = ((), (), s32[]{:S(2)}) async-start(), calls=%async_computation.6 | async-start | bytes 4194304 | tf_op jit(solution)/shard_map/psum | solution.py:13
  10.5 32.0 %copy-start.8 = (f32[16,512]{1,0:T(8,128)S(1)}, f32[16,512]{1,0:T(8,128)}, u32[]{:S(2)}) copy-start(f32[16,512]{1,0:T(8,128)} %param.12) | copy-start | bytes 98308
  68.3 148.9 %copy-start.3 = (f32[256,512]{1,0:T(8,128)S(1)}, f32[256,512]{1,0:T(8,128)}, u32[]{:S(2)}) copy-start(f32[256,512]{1,0:T(8,128)} %param.8) | copy-start | bytes 1572868
  68.3 209.8 %reduce-scatter.3.cloned.1.call-start = ((), (), s32[]{:S(2)}) async-start(), calls=%async_computation.2 | async-start | bytes 557056 | tf_op jit(solution)/shard_map/reduce_scatter | solution.py:65
  220.3 0.8 copy-start.9
  220.3 2.0 copy-start.5
  220.3 129.4 %all-gather.2.cloned.1.call-start = ((), (), s32[]{:S(2)}) async-start(), calls=%async_computation.4 | async-start | bytes 1081344 | tf_op jit(solution)/shard_map/all_gather | solution.py:34
  222.3 187.5 %reduce-scatter.5.cloned.1.call-start = ((), (), s32[]{:S(2)}) async-start(), calls=%async_computation.3 | async-start | bytes 557056 | tf_op jit(solution)/shard_map/reduce_scatter | solution.py:65
  225.3 684.5 %all-reduce.5.cloned.1.call-start = ((), (), s32[]{:S(2)}) async-start(), calls=%async_computation.5 | async-start | bytes 6291456 | tf_op jit(solution)/shard_map/psum | solution.py:79
  279.0 130.9 %copy-start.6 = (f32[16,512]{1,0:T(8,128)}, f32[16,512]{1,0:T(8,128)S(1)}, u32[]{:S(2)}) copy-start(f32[16,512]{1,0:T(8,128)S(1)} %multiply_negate_fusion.1) | copy-start | bytes 98308
  412.3 2.0 copy-start.7
  909.8 3.9 copy-start.2
  909.8 3.9 copy-start.4
Sparse Core Ops, SparseCore 0:
  68.4 148.7 all-reduce.6
  220.4 57.6 reduce-scatter.2
  282.3 67.3 all-gather.1
  352.6 57.1 reduce-scatter.4
  416.5 493.2 all-reduce.4
where the time goes:
time: 927 us; the launch traced here: 926 us
  waiting for transfers between devices  824 us (89%)
  blocking collectives  54.9 us (6%)
  matrix products  27.4 us (3%)
  between operations  13.9 us (1%)
    psum x1, waiting for transfers between devices, shards(): diag_one = gram_one + lax.psum(one_partial, ('row', 'col'))  493 us
    psum x1, waiting for transfers between devices, spread_2(): return lax.psum(kept, axis)  149 us
    reduce_scatter x2, waiting for transfers between devices, single_reduce(): lax.psum_scatter(make(jnp.int32(0), rows_dev // col_count * lax.axis_size...  113 us
    all_gather x1, waiting for transfers between devices, shards(): lax.all_gather(product(l_pair, linv_two), 'row', axis=0, tiled=True)  68.8 us
    all_gather x2, blocking collectives, spread(): near = lax.all_gather(u_fine, 'col', axis=0, tiled=True)  54.9 us
  transfers between devices with their start and end apart: 5, of which 5 were waited for; matrix products, arithmetic and copies ran while one was open for 1% of the time, Pallas kernels for 0%

commit v1 on v0

v1 whole, which is shorter than its diff:
```python
import functools

import jax
import jax.numpy as jnp
from jax import lax
from jax.experimental import pallas as pl
from jax.experimental.pallas import tpu as pltpu
from jax.sharding import PartitionSpec as P

BLK = 128
FINE = 16
MESH = pl.DeviceIdType.MESH
F32 = jnp.float32
BF16 = jnp.bfloat16


def split(value):
    high = value.astype(BF16)
    low = (value - high.astype(F32)).astype(BF16)
    return high, low


def dot_parts(a, b, dims):
    def one(left, right):
        return lax.dot_general(left, right, (dims, ((), ())), preferred_element_type=F32)

    return one(a[0], b[0]) + (one(a[0], b[1]) + one(a[1], b[0]))


def nn(a, b):
    return dot_parts(split(a), b, ((1,), (0,)))


def nt(a, b):
    return dot_parts(split(a), b, ((1,), (1,)))


def kernel(
    side,
    in_one, in_two, l_one, l_two, l_pair, z_hbm, linv_one_hbm, linv_two_hbm,
    col_one, diag_one, col_two, pair_block, diag_two,
    z_v, linv_one, linv_two, own, hop, far, near, res, m_high, m_low, part, ring, pack, got,
    local_sem, hop_recv, far_recv, send_sem, first_recv, second_recv, core_recv, ring_send, ring_recv, got_sem,
):
    chips = side * side
    zn = chips
    width = l_one.shape[1]
    row = lax.axis_index("row")
    col = lax.axis_index("col")
    core = lax.rem(row, 2)
    chip = lax.div(row, 2)
    x = lax.div(chip, side)
    y = lax.rem(chip, side)
    sibling = row + 1 - 2 * core

    def local(source, target, sem):
        return pltpu.make_async_copy(source, target, sem)

    def send(source, target, s_sem, r_sem, device):
        pltpu.make_async_remote_copy(
            src_ref=source, dst_ref=target, send_sem=s_sem, recv_sem=r_sem,
            device_id=device, device_id_type=MESH,
        ).start()

    def arrived(ref, sem):
        pltpu.make_async_copy(ref, ref, sem).wait()

    staged = [
        local(z_hbm, z_v, local_sem.at[0]),
        local(linv_one_hbm, linv_one, local_sem.at[1]),
        local(linv_two_hbm, linv_two, local_sem.at[2]),
    ]
    for copy in staged:
        copy.start()

    barrier = pltpu.get_barrier_semaphore()

    def greet(device):
        pl.semaphore_signal(barrier, inc=1, device_id=device, device_id_type=MESH)

    greet((sibling, col))
    for step in range(1, chips):
        greet((2 * lax.rem(chip + step, chips) + core, col))
    for step in range(1, zn):
        greet((row, lax.rem(col + step, zn)))

    block = lax.div(row * (zn * FINE) + col * FINE, BLK)
    flag_one = in_one[block].astype(F32)
    flag_two = in_two[block].astype(F32)
    mine_one = l_one[...] * flag_one
    mine_two = l_two[...] * flag_two
    here = core * chips + chip
    near[here, :, :width] = mine_one
    near[here, :, width:2 * width] = mine_two
    near[here, :, 2 * width:] = l_pair[...]
    tiles = width // 128
    for tile in range(2 * tiles):
        source = mine_one if tile < tiles else mine_two
        at = (tile % tiles) * 128
        for half in range(2):
            own[2 * tile + half] = source[8 * half:8 * half + 8, at:at + 128]

    pl.semaphore_wait(barrier, chips + zn - 1)

    mine = local(own.at[chip], hop.at[chip], hop_recv.at[chip])
    mine.start()
    for step in range(1, chips):
        to = lax.rem(chip + step, chips)
        send(own.at[to], hop.at[chip], send_sem.at[0], hop_recv.at[chip], (2 * to + core, col))
    for step in range(1, zn):
        to = lax.rem(col + step, zn)
        arrived(hop.at[to], hop_recv.at[to])
        send(hop.at[to], far.at[here, col], send_sem.at[1], far_recv, (row, to))
    arrived(hop.at[col], hop_recv.at[col])
    far[here, col] = hop[col]

    def place(first, second, which):
        xs = lax.rem(x + side + first * (1 - which) + second * which, side)
        ys = lax.rem(y + side + first * which + second * (1 - which), side)
        return xs * side + ys

    def peer(first, second):
        return (2 * place(first, second, core) + core, col)

    def spread_first(buf, which):
        for d in range(1, side):
            send(buf.at[here], buf.at[here], send_sem.at[2 + which], first_recv.at[which, d], peer(d, 0))

    def spread_second(buf, which):
        for e in range(side):
            spot = core * chips + place(-e, 0, core)
            if e:
                arrived(buf.at[spot], first_recv.at[which, e])
            for d in range(1, side):
                send(buf.at[spot], buf.at[spot], send_sem.at[2 + which], second_recv.at[which, e, d], peer(0, d))
            send(buf.at[spot], buf.at[spot], send_sem.at[2 + which], core_recv.at[which], (sibling, col))

    def spread_third(buf, which):
        for d in range(1, side):
            for e in range(side):
                spot = core * chips + place(-e, -d, core)
                arrived(buf.at[spot], second_recv.at[which, e, d])
                send(buf.at[spot], buf.at[spot], send_sem.at[2 + which], core_recv.at[which], (sibling, col))

    def spread_end(buf, which):
        arrived(buf.at[pl.ds((1 - core) * chips, chips)], core_recv.at[which])

    staged[0].wait()
    z_parts = split(z_v[...])
    arrived(far.at[0, pl.ds(0, zn - 1)], far_recv)
    spread_first(far, 0)
    spread_second(far, 0)
    spread_third(far, 0)
    spread_end(far, 0)
    spread_first(near, 1)

    for which in range(2):
        for tile in range(2 * tiles):
            at = which * chips + 2 * tile
            value = jnp.stack([far[at], far[at + 1]], axis=1).reshape(zn * FINE, 128)
            high, low = split(value)
            rows = slice(which * zn * FINE, (which + 1) * zn * FINE)
            m_high[rows, tile * 128:tile * 128 + 128] = high
            m_low[rows, tile * 128:tile * 128 + 128] = low

    most = zn // 2
    steps = ((most, most - 1), (most - 1, most))
    up = lax.rem(col + 1, zn)
    down = lax.rem(col + zn - 1, zn)

    def ring_step(half, way, step):
        count = steps[half][way]
        if step >= count:
            return
        owner = lax.rem(col + zn + (count - step if way == 0 else step - count), zn)
        if step == 0:
            source = part.at[half, owner]
        else:
            source = ring.at[half, way, step - 1]
            arrived(source, ring_recv.at[half, way, step - 1])
            ring[half, way, step - 1] = ring[half, way, step - 1] + part[half, owner]
        send(source, ring.at[half, way, step], ring_send.at[half, way], ring_recv.at[half, way, step],
             (row, up if way == 0 else down))

    for half in range(2):
        cols = slice(half * width, (half + 1) * width)
        product = dot_parts(z_parts, (m_high[:, cols], m_low[:, cols]), ((1,), (0,)))
        part[half] = product.reshape(zn, FINE, width)
        for way in range(2):
            ring_step(half, way, 0)

    for step in range(1, most):
        for half in range(2):
            for way in range(2):
                ring_step(half, way, step)
        if step == min(2, most - 1):
            spread_second(near, 1)
        if step == min(4, most - 1):
            spread_third(near, 1)

    staged[1].wait()
    staged[2].wait()
    inv_one = split(linv_one[...])
    inv_two = split(linv_two[...])
    spread_end(near, 1)
    count = 2 * chips * FINE
    near_one = split(near[:, :, :width].reshape(count, width))
    near_two = split(near[:, :, width:2 * width].reshape(count, width))
    pair = jnp.concatenate(
        [near[which * chips + t, :, 2 * width:] for t in range(chips) for which in range(2)], axis=0
    )
    pair = split(pair)
    line = lax.broadcasted_iota(jnp.int32, (48, width), 0)
    lane = lax.broadcasted_iota(jnp.int32, (48, width), 1)
    wanted = jnp.where(line < 16, row * 16 + line, col * 32 + line - 16)
    pick = jnp.where(lane == wanted, 1.0, 0.0).astype(F32)
    tri_one = nt(pick, inv_one)
    tri_two = nt(pick, inv_two)
    tri_pair = nt(nt(tri_two, pair), inv_one)
    u_one_t = nt(tri_one[:16], near_one)
    u_two_t = nt(tri_two[:16], near_two)
    q_t = nt(tri_pair[:16], near_one)
    gram_one = nt(tri_one[:16], split(tri_one[16:]))
    gram_pair = nt(tri_one[:16], split(tri_pair[16:]))
    gram_two = nt(tri_two[:16], split(tri_two[16:])) + nt(tri_pair[:16], split(tri_pair[16:]))

    for half in range(2):
        ends = []
        for way in range(2):
            last = steps[half][way] - 1
            arrived(ring.at[half, way, last], ring_recv.at[half, way, last])
            ends.append(ring[half, way, last])
        res[here, :, half * width:(half + 1) * width] = part[half, col] + ends[0] + ends[1]

    spread_first(res, 2)
    y_one = nn(res[here, :, :width], inv_one)
    one = -(flag_one * y_one)
    col_one[...] = one
    spread_second(res, 2)
    y_two = nn(res[here, :, width:] + nn(one, pair), inv_two)
    col_two[...] = -(flag_two * y_two)
    spread_third(res, 2)
    spread_end(res, 2)

    res_one = split(res[:, :, :width].reshape(count, width))
    res_two = split(res[:, :, width:].reshape(count, width))
    a = nn(jnp.concatenate([u_one_t, u_two_t, q_t], axis=0), res_one)
    b = nn(u_two_t, res_two)
    y_t = nt(jnp.concatenate([tri_one[:16], tri_pair[:16]], axis=0), res_one)
    c = nn(y_t, near_two)
    d = nn(jnp.concatenate([a[:16], a[32:] - a[16:32]], axis=0), inv_one)
    e = nn(d, pair) + jnp.concatenate([-c[:16], b - c[16:]], axis=0)
    s = nn(e, inv_two)
    sums = (d[:16], s[:16], s[16:])

    lanes = lax.broadcasted_iota(jnp.int32, (FINE, 128), 1)
    for owner in range(zn):
        at = (owner // 4) * 128
        packed = jnp.zeros((FINE, 128), F32)
        for n in range(3):
            piece = sums[n][:, at:at + 128]
            shift = (32 * n - 32 * (owner % 4)) % 128
            if shift:
                piece = pltpu.roll(piece, shift, 1)
            packed = jnp.where((lanes >= 32 * n) & (lanes < 32 * n + 32), piece, packed)
        pack[owner] = packed
    for step in range(1, zn):
        to = lax.rem(col + step, zn)
        send(pack.at[to], got.at[step], got_sem.at[0], got_sem.at[1], (row, to))
    arrived(got.at[pl.ds(1, zn - 1)], got_sem.at[1])
    total = pack[col]
    for step in range(1, zn):
        total = total + got[step]
    diag_one[...] = total[:, :32] + gram_one
    pair_block[...] = -(pltpu.roll(total, 96, 1)[:, :32] + gram_pair)
    diag_two[...] = pltpu.roll(total, 64, 1)[:, :32] + gram_two

    arrived(own.at[pl.ds(0, chips - 1)], send_sem.at[0])
    arrived(hop.at[pl.ds(0, zn - 1)], send_sem.at[1])
    for which, buf in enumerate((far, near, res)):
        arrived(buf.at[pl.ds(0, 2 * chips - 1)], send_sem.at[2 + which])
    for half in range(2):
        for way in range(2):
            arrived(part.at[half, pl.ds(0, steps[half][way])], ring_send.at[half, way])
    arrived(got.at[pl.ds(1, zn - 1)], got_sem.at[0])


def shards(side, z_anc, in_one, in_two, l_one, l_two, l_pair, linv_one, linv_two):
    width = l_one.shape[1]
    chips = side * side
    zn = chips
    rows, depth = z_anc.shape
    vmem = pl.BlockSpec(memory_space=pltpu.VMEM)
    smem = pl.BlockSpec(memory_space=pltpu.SMEM)
    hbm = pl.BlockSpec(memory_space=pl.ANY)
    dma = pltpu.SemaphoreType.DMA
    out = lambda *shape: jax.ShapeDtypeStruct(shape, F32)
    return tuple(pl.pallas_call(
        functools.partial(kernel, side),
        out_shape=(
            out(FINE, width), out(16, 32), out(FINE, width), out(16, 32), out(16, 32),
        ),
        in_specs=[smem, smem, vmem, vmem, vmem, hbm, hbm, hbm],
        out_specs=[vmem] * 5,
        scratch_shapes=[
            pltpu.VMEM((rows, depth), F32),
            pltpu.VMEM((width, width), F32),
            pltpu.VMEM((width, width), F32),
            pltpu.VMEM((chips, 8, 128), F32),
            pltpu.VMEM((chips, 8, 128), F32),
            pltpu.VMEM((2 * chips, zn, 8, 128), F32),
            pltpu.VMEM((2 * chips, FINE, 3 * width), F32),
            pltpu.VMEM((2 * chips, FINE, 2 * width), F32),
            pltpu.VMEM((depth, 2 * width), BF16),
            pltpu.VMEM((depth, 2 * width), BF16),
            pltpu.VMEM((2, zn, FINE, width), F32),
            pltpu.VMEM((2, 2, zn // 2, FINE, width), F32),
            pltpu.VMEM((zn, FINE, 128), F32),
            pltpu.VMEM((zn, FINE, 128), F32),
            dma((3,)),
            dma((chips,)),
            dma,
            dma((5,)),
            dma((3, side)),
            dma((3, side, side)),
            dma((3,)),
            dma((2, 2)),
            dma((2, 2, zn // 2)),
            dma((2,)),
        ],
        compiler_params=pltpu.CompilerParams(
            collective_id=0, has_side_effects=True, vmem_limit_bytes=48 * 1024 * 1024
        ),
    )(in_one, in_two, l_one, l_two, l_pair, z_anc, linv_one, linv_two))


def solution(mesh):
    side = 1
    while side * side < mesh.shape["col"]:
        side += 1
    placed = (
        P("row", "col"),
        P(),
        P(),
        P(("row", "col"), None),
        P(("row", "col"), None),
        P("row", None),
        P(),
        P(),
    )
    return jax.shard_map(
        functools.partial(shards, side),
        mesh=mesh,
        in_specs=placed,
        out_specs=(
            P(("row", "col"), None),
            P("row", "col"),
            P(("row", "col"), None),
            P("row", "col"),
            P("row", "col"),
        ),
        check_vma=False,
    )
```

time: 927 us -> 112 us (0.12)
  waiting for transfers between devices: 824 us -> 0 us
  Pallas kernels: 0 us -> 101 us
  blocking collectives: 54.9 us -> 0 us
  matrix products: 27.4 us -> 0 us
  between operations: 13.9 us -> 0.66 us
    psum x2 -> x0, waiting for transfers between devices: 642 us -> none  [the longest x1 493 us: shards(): diag_one = gram_one + lax.psum(one_partial, ('row', 'col'))]
    reduce_scatter x2 -> x0, waiting for transfers between devices: 113 us -> none  [single_reduce(): lax.psum_scatter(make(jnp.int32(0), rows_dev // col_count * lax.axis_size...]
    pallas_call x0 -> x1, Pallas kernels: none -> 101 us  [shards(): pl.pallas_call(functools.partial(kernel, side), out_shape=(out(FINE, widt...]
    all_gather x1 -> x0, waiting for transfers between devices: 68.8 us -> none  [shards(): lax.all_gather(product(l_pair, linv_two), 'row', axis=0, tiled=True)]
    all_gather x2 -> x0, blocking collectives: 54.9 us -> none  [spread(): near = lax.all_gather(u_fine, 'col', axis=0, tiled=True)]
    dot_general x15 -> x0, matrix products: 27.4 us -> none  [the longest x2 6 us: make_rows(): return product(z_anc, far_all)]
    unnamed x20 -> x21, local copies, waits for them, and re-layouts: 0.71 us -> 10.1 us
  transfers between devices with their start and end apart: 5 -> 0, of which waited for: 5 -> 0; matrix products, arithmetic and copies ran while one was open for 1% -> 0% of each run, Pallas kernels for 0% -> 0%
where the time goes in v1:
time: 112 us
  Pallas kernels  101 us (90%)
  local copies, waits for them, and re-layouts  10.1 us (9%)
    pallas_call x1, Pallas kernels, shards(): pl.pallas_call(functools.partial(kernel, side), out_shape=(out(FINE, widt...  101 us
    unnamed x21, local copies, waits for them, and re-layouts  10.1 us

profile of v1, /device:TPU:1, one launch (start us, length us, event | category | flops | bytes accessed | tf_op | source)
XLA Modules:
  0.0 111.5 jit_solution(3947406875609924112)
XLA Ops:
  0.6 0.0 copy-start
  0.6 1.2 %copy-done = f32[512,512]{1,0:T(8,128)S(1)} copy-done((f32[512,512]{1,0:T(8,128)S(1)}, f32[512,512]{1,0:T(8,128)}, u32[]{:S(2)}) %copy-start) | copy-done | bytes 1048600
  1.9 0.0 copy-start.1
  1.9 1.2 %copy-done.1 = f32[512,512]{1,0:T(8,128)S(1)} copy-done((f32[512,512]{1,0:T(8,128)S(1)}, f32[512,512]{1,0:T(8,128)}, u32[]{:S(2)}) %copy-start.1) | copy-done | bytes 1048600
  3.1 0.0 copy-start.2
  3.1 1.0 copy-done.2
  4.1 0.0 copy-start.3
  4.1 0.8 copy-done.3
  4.9 0.0 copy-start.4
  4.9 0.8 copy-done.4
  5.6 0.0 copy-start.5
  5.6 0.8 copy-done.5
  6.4 0.0 copy-start.6
  6.4 0.7 copy-done.6
  7.1 0.0 copy-start.7
  7.1 0.7 copy-done.7
  7.7 100.8 %shard_map.119 = (f32[16,512]{1,0:T(8,128)S(1)}, f32[16,32]{1,0:T(8,128)S(1)}, f32[16,512]{1,0:T(8,128)S(1)}, f32[16,32]{1,0:T(8,128)S(1)}, f32[16,32]{1,0:T(8,128)S(1)}) custom-call(s32[64]{0:T(128)S(1)} %copy-done.6, s32[64]{0:T(128)S(1)} %copy-done.7, f32[16,512]{1,0:T(8,128)S(1)} %copy-done.3, f32[16,512]{1,0:T(8,128)S(1)} %copy-done.4, ...), custom_call_target="tpu_custom_call" | custom-call | tf_op jit(solution)/shard_map/pallas_call | solution.py:298
  108.5 0.6 copy.18
  109.1 0.6 copy.19
  109.7 0.6 copy.20
  110.3 0.6 copy.21
  110.9 0.6 copy.22
Async XLA Ops:
  0.6 1.2 %copy-start = (f32[512,512]{1,0:T(8,128)S(1)}, f32[512,512]{1,0:T(8,128)}, u32[]{:S(2)}) copy-start(f32[512,512]{1,0:T(8,128)} %linv_one_hbm.1) | copy-start | bytes 3145732
  1.9 1.2 %copy-start.1 = (f32[512,512]{1,0:T(8,128)S(1)}, f32[512,512]{1,0:T(8,128)}, u32[]{:S(2)}) copy-start(f32[512,512]{1,0:T(8,128)} %linv_two_hbm.1) | copy-start | bytes 3145732
  3.1 1.0 copy-start.2
  4.1 0.8 copy-start.3
  4.9 0.8 copy-start.4
  5.6 0.8 copy-start.5
  6.4 0.7 copy-start.6
  7.1 0.7 copy-start.7

commit v2 on v1

v2 whole, which is shorter than its diff:
```python
import functools

import jax
import jax.numpy as jnp
from jax import lax
from jax.experimental import pallas as pl
from jax.experimental.pallas import tpu as pltpu
from jax.sharding import PartitionSpec as P

BLK = 128
FINE = 16
MESH = pl.DeviceIdType.MESH
F32 = jnp.float32
BF16 = jnp.bfloat16


def split(value):
    high = value.astype(BF16)
    low = (value - high.astype(F32)).astype(BF16)
    return high, low


def dot_parts(a, b, dims):
    def one(left, right):
        return lax.dot_general(left, right, (dims, ((), ())), preferred_element_type=F32)

    return one(a[0], b[0]) + (one(a[0], b[1]) + one(a[1], b[0]))


def nn(a, b):
    return dot_parts(split(a), b, ((1,), (0,)))


def nt(a, b):
    return dot_parts(split(a), b, ((1,), (1,)))


def kernel(
    side, pieces,
    in_one_hbm, in_two_hbm, l_one_hbm, l_two_hbm, l_pair_hbm, z_hbm, linv_one_hbm, linv_two_hbm,
    col_one, diag_one, col_two, pair_block, diag_two,
    in_one, in_two, l_one, l_two, l_pair, z_v, linv_one, linv_two,
    own, hop, far, near, res, m_high, m_low, part, even, odd, pack, got,
    local_sem, hop_recv, far_recv, send_sem, first_recv, second_recv, core_recv, tree_send, even_recv, odd_recv, got_sem,
):
    chips = side * side
    zn = chips
    width = l_one.shape[1]
    row = lax.axis_index("row")
    col = lax.axis_index("col")
    core = lax.rem(row, 2)
    chip = lax.div(row, 2)
    x = lax.div(chip, side)
    y = lax.rem(chip, side)
    sibling = row + 1 - 2 * core
    here = core * chips + chip

    def send(source, target, s_sem, r_sem, device):
        pltpu.make_async_remote_copy(
            src_ref=source, dst_ref=target, send_sem=s_sem, recv_sem=r_sem,
            device_id=device, device_id_type=MESH,
        ).start()

    def arrived(ref, sem):
        pltpu.make_async_copy(ref, ref, sem).wait()

    staged = [
        pltpu.make_async_copy(source, target, local_sem.at[n])
        for n, (source, target) in enumerate((
            (in_one_hbm, in_one), (in_two_hbm, in_two), (l_one_hbm, l_one), (l_two_hbm, l_two),
            (l_pair_hbm, l_pair), (z_hbm, z_v), (linv_one_hbm, linv_one), (linv_two_hbm, linv_two),
        ))
    ]
    for copy in staged:
        copy.start()

    barrier = pltpu.get_barrier_semaphore()

    def greet(device):
        pl.semaphore_signal(barrier, inc=1, device_id=device, device_id_type=MESH)

    for step in sorted(range(1, zn), key=lambda n: -min(n, zn - n)):
        greet((row, lax.rem(col + step, zn)))
    for step in range(1, chips):
        greet((2 * lax.rem(chip + step, chips) + core, col))
    greet((sibling, col))

    for copy in staged[:5]:
        copy.wait()
    block = lax.div(row * (zn * FINE) + col * FINE, BLK)
    flag_one = in_one[block].astype(F32)
    flag_two = in_two[block].astype(F32)
    mine_one = l_one[...] * flag_one
    mine_two = l_two[...] * flag_two
    near[here, :, :width] = mine_one
    near[here, :, width:2 * width] = mine_two
    near[here, :, 2 * width:] = l_pair[...]
    tiles = width // 128
    for tile in range(2 * tiles):
        source = mine_one if tile < tiles else mine_two
        at = (tile % tiles) * 128
        for half in range(2):
            own[2 * tile + half] = source[8 * half:8 * half + 8, at:at + 128]

    group = zn // 2
    lead = zn // 4
    staged[5].wait()
    turn = lax.rem(lead * FINE + (zn - col) * FINE, zn * FINE)
    depth = zn * FINE
    z_parts = split(jnp.concatenate(
        [pltpu.roll(z_v[:, n * depth:(n + 1) * depth], turn, 1) for n in range(2)], axis=1
    ))

    pl.semaphore_wait(barrier, chips + zn - 1)

    mine = pltpu.make_async_copy(own.at[chip], hop.at[chip], hop_recv.at[chip])
    mine.start()
    for step in range(1, chips):
        to = lax.rem(chip + step, chips)
        send(own.at[to], hop.at[chip], send_sem.at[0], hop_recv.at[chip], (2 * to + core, col))
    for step in sorted(range(1, zn), key=lambda n: -min(n, zn - n)):
        to = lax.rem(col + step, zn)
        spot = (lead - step) % zn
        arrived(hop.at[to], hop_recv.at[to])
        send(hop.at[to], far.at[here, spot], send_sem.at[1], far_recv.at[spot // group], (row, to))
    arrived(hop.at[col], hop_recv.at[col])
    far[here, lead] = hop[col]

    def place(first, second, which):
        xs = lax.rem(x + side + first * (1 - which) + second * which, side)
        ys = lax.rem(y + side + first * which + second * (1 - which), side)
        return xs * side + ys

    def peer(first, second):
        return (2 * place(first, second, core) + core, col)

    def spread_first(view, sem, which):
        for d in range(1, side):
            send(view(here), view(here), send_sem.at[sem], first_recv.at[which, d], peer(d, 0))

    def spread_second(view, sem, which):
        for e in range(side):
            spot = core * chips + place(-e, 0, core)
            if e:
                arrived(view(spot), first_recv.at[which, e])
            for d in range(1, side):
                send(view(spot), view(spot), send_sem.at[sem], second_recv.at[which, e, d], peer(0, d))
            send(view(spot), view(spot), send_sem.at[sem], core_recv.at[which], (sibling, col))

    def spread_third(view, sem, which):
        for d in range(1, side):
            for e in range(side):
                spot = core * chips + place(-e, -d, core)
                arrived(view(spot), second_recv.at[which, e, d])
                send(view(spot), view(spot), send_sem.at[sem], core_recv.at[which], (sibling, col))

    def spread_end(view, which):
        arrived(view(pl.ds((1 - core) * chips, chips)), core_recv.at[which])

    def far_half(n):
        return lambda spot: far.at[spot, pl.ds(n * group, group)]

    def near_all(spot):
        return near.at[spot]

    def res_half(n):
        return lambda spot: res.at[n, spot]

    arrived(far.at[0, pl.ds(0, group - 1)], far_recv.at[0])
    spread_first(far_half(0), 2, 0)
    arrived(far.at[0, pl.ds(0, group)], far_recv.at[1])
    spread_first(far_half(1), 2, 1)
    spread_second(far_half(0), 2, 0)
    spread_second(far_half(1), 2, 1)
    spread_third(far_half(0), 2, 0)
    spread_third(far_half(1), 2, 1)
    spread_end(far_half(0), 0)
    spread_end(far_half(1), 1)
    spread_first(near_all, 3, 2)

    for which in range(2):
        for tile in range(2 * tiles):
            at = which * chips + 2 * tile
            value = jnp.stack([far[at], far[at + 1]], axis=1).reshape(depth, 128)
            high, low = split(value)
            rows = slice(which * depth, (which + 1) * depth)
            m_high[rows, tile * 128:tile * 128 + 128] = high
            m_low[rows, tile * 128:tile * 128 + 128] = low

    most = zn // 2
    ways = (0, 1)

    def reach(piece, way):
        return most if (piece + way) % 2 == 0 else most - 1

    def along(way, distance):
        return lax.rem(col + (distance if way == 0 else zn - distance), zn)

    def leaf(piece, way, distance):
        if distance > reach(piece, way):
            return
        source = part.at[piece, along(way, distance)]
        level = (distance - 1) // 2
        if distance % 2:
            send(source, odd.at[piece, way, level], tree_send.at[piece, way], odd_recv.at[piece, way, level],
                 (row, along(way, 1)))
        else:
            send(source, even.at[piece, way, level], tree_send.at[piece, way], even_recv.at[piece, way, level],
                 (row, along(way, 2)))

    def gathered(piece, way, distance):
        level = distance // 2
        arrived(odd.at[piece, way, level], odd_recv.at[piece, way, level])
        total = odd[piece, way, level]
        if distance + 2 <= reach(piece, way):
            arrived(even.at[piece, way, level], even_recv.at[piece, way, level])
            total = total + even[piece, way, level]
        return total

    def chain(piece, way, distance):
        if distance + 1 > reach(piece, way):
            leaf(piece, way, distance)
            return
        level = distance // 2
        odd[piece, way, level] = part[piece, along(way, distance)] + gathered(piece, way, distance)
        send(odd.at[piece, way, level], even.at[piece, way, level - 1], tree_send.at[piece, way],
             even_recv.at[piece, way, level - 1], (row, along(way, 2)))

    share = 2 * width // pieces
    for piece in range(pieces):
        cols = slice(piece * share, (piece + 1) * share)
        product = dot_parts(z_parts, (m_high[:, cols], m_low[:, cols]), ((1,), (0,)))
        part[piece] = product.reshape(zn, FINE, share)
        for way in ways:
            leaf(piece, way, most)
            leaf(piece, way, most - 1)
    if most > 3:
        for piece in range(pieces):
            for way in ways:
                leaf(piece, way, most - 3)

    for distance in range(most - 2, 0, -2):
        for piece in range(pieces):
            for way in ways:
                chain(piece, way, distance)
        if distance > 3:
            for piece in range(pieces):
                for way in ways:
                    leaf(piece, way, distance - 3)
        if distance == most - 2:
            spread_second(near_all, 3, 2)
        if distance == max(most - 4, 2):
            spread_third(near_all, 3, 2)
    if most <= 2:
        spread_second(near_all, 3, 2)
        spread_third(near_all, 3, 2)

    for copy in staged[6:]:
        copy.wait()
    inv_one = split(linv_one[...])
    inv_two = split(linv_two[...])
    spread_end(near_all, 2)
    count = 2 * chips * FINE
    near_one = split(near[:, :, :width].reshape(count, width))
    near_two = split(near[:, :, width:2 * width].reshape(count, width))
    pair = jnp.concatenate(
        [near[which * chips + t, :, 2 * width:] for t in range(chips) for which in range(2)], axis=0
    )
    pair = split(pair)
    line = lax.broadcasted_iota(jnp.int32, (48, width), 0)
    lane = lax.broadcasted_iota(jnp.int32, (48, width), 1)
    wanted = jnp.where(line < 16, row * 16 + line, col * 32 + line - 16)
    pick = jnp.where(lane == wanted, 1.0, 0.0).astype(F32)
    tri_one = nt(pick, inv_one)
    tri_two = nt(pick, inv_two)
    tri_pair = nt(nt(tri_two, pair), inv_one)
    u_one_t = nt(tri_one[:16], near_one)
    u_two_t = nt(tri_two[:16], near_two)
    q_t = nt(tri_pair[:16], near_one)
    gram_one = nt(tri_one[:16], split(tri_one[16:]))
    gram_pair = nt(tri_one[:16], split(tri_pair[16:]))
    gram_two = nt(tri_two[:16], split(tri_two[16:])) + nt(tri_pair[:16], split(tri_pair[16:]))

    for piece in range(pieces):
        sums = [gathered(piece, way, 0) for way in ways]
        at = piece * share % width
        n = piece * share // width
        res[n, here, :, at:at + share] = part[piece, col] + sums[0] + sums[1]
        if at + share == width:
            spread_first(res_half(n), 4, 3 + n)

    y_one = nn(res[0, here], inv_one)
    one = -(flag_one * y_one)
    col_one[...] = one
    spread_second(res_half(0), 4, 3)
    spread_second(res_half(1), 4, 4)
    y_two = nn(res[1, here] + nn(one, pair), inv_two)
    col_two[...] = -(flag_two * y_two)
    spread_third(res_half(0), 4, 3)
    spread_third(res_half(1), 4, 4)
    spread_end(res_half(0), 3)

    res_one = split(res[0].reshape(count, width))
    a = nn(jnp.concatenate([u_one_t, u_two_t, q_t], axis=0), res_one)
    y_t = nt(jnp.concatenate([tri_one[:16], tri_pair[:16]], axis=0), res_one)
    c = nn(y_t, near_two)
    d = nn(jnp.concatenate([a[:16], a[32:] - a[16:32]], axis=0), inv_one)
    e = nn(d, pair)
    spread_end(res_half(1), 4)
    b = nn(u_two_t, split(res[1].reshape(count, width)))
    s = nn(e + jnp.concatenate([-c[:16], b - c[16:]], axis=0), inv_two)
    sums = (d[:16], s[:16], s[16:])

    lanes = lax.broadcasted_iota(jnp.int32, (FINE, 128), 1)
    for owner in range(zn):
        at = (owner // 4) * 128
        packed = jnp.zeros((FINE, 128), F32)
        for n in range(3):
            piece = sums[n][:, at:at + 128]
            shift = (32 * n - 32 * (owner % 4)) % 128
            if shift:
                piece = pltpu.roll(piece, shift, 1)
            packed = jnp.where((lanes >= 32 * n) & (lanes < 32 * n + 32), piece, packed)
        pack[owner] = packed
    for step in sorted(range(1, zn), key=lambda n: -min(n, zn - n)):
        to = lax.rem(col + step, zn)
        send(pack.at[to], got.at[step], got_sem.at[0], got_sem.at[1], (row, to))
    arrived(got.at[pl.ds(1, zn - 1)], got_sem.at[1])
    total = pack[col]
    for step in range(1, zn):
        total = total + got[step]
    diag_one[...] = total[:, :32] + gram_one
    pair_block[...] = -(pltpu.roll(total, 96, 1)[:, :32] + gram_pair)
    diag_two[...] = pltpu.roll(total, 64, 1)[:, :32] + gram_two

    arrived(own.at[pl.ds(0, chips - 1)], send_sem.at[0])
    arrived(hop.at[pl.ds(0, zn - 1)], send_sem.at[1])
    arrived(far.at[pl.ds(0, 2 * chips - 1)], send_sem.at[2])
    arrived(near.at[pl.ds(0, 2 * chips - 1)], send_sem.at[3])
    for n in range(2):
        arrived(res.at[n, pl.ds(0, 2 * chips - 1)], send_sem.at[4])
    for piece in range(pieces):
        for way in ways:
            arrived(part.at[piece, pl.ds(0, reach(piece, way))], tree_send.at[piece, way])
    arrived(got.at[pl.ds(1, zn - 1)], got_sem.at[0])


def shards(side, z_anc, in_one, in_two, l_one, l_two, l_pair, linv_one, linv_two):
    width = l_one.shape[1]
    chips = side * side
    zn = chips
    rows, depth = z_anc.shape
    pieces = 4 if width > 128 else 2
    share = 2 * width // pieces
    levels = zn // 4
    vmem = pl.BlockSpec(memory_space=pltpu.VMEM)
    hbm = pl.BlockSpec(memory_space=pl.ANY)
    dma = pltpu.SemaphoreType.DMA
    out = lambda *shape: jax.ShapeDtypeStruct(shape, F32)
    held = lambda array: pltpu.VMEM(array.shape, array.dtype)
    return tuple(pl.pallas_call(
        functools.partial(kernel, side, pieces),
        out_shape=(
            out(FINE, width), out(16, 32), out(FINE, width), out(16, 32), out(16, 32),
        ),
        in_specs=[hbm] * 8,
        out_specs=[vmem] * 5,
        scratch_shapes=[
            pltpu.SMEM(in_one.shape, in_one.dtype),
            pltpu.SMEM(in_two.shape, in_two.dtype),
            held(l_one), held(l_two), held(l_pair), held(z_anc), held(linv_one), held(linv_two),
            pltpu.VMEM((chips, 8, 128), F32),
            pltpu.VMEM((chips, 8, 128), F32),
            pltpu.VMEM((2 * chips, zn, 8, 128), F32),
            pltpu.VMEM((2 * chips, FINE, 3 * width), F32),
            pltpu.VMEM((2, 2 * chips, FINE, width), F32),
            pltpu.VMEM((depth, 2 * width), BF16),
            pltpu.VMEM((depth, 2 * width), BF16),
            pltpu.VMEM((pieces, zn, FINE, share), F32),
            pltpu.VMEM((pieces, 2, levels, FINE, share), F32),
            pltpu.VMEM((pieces, 2, levels, FINE, share), F32),
            pltpu.VMEM((zn, FINE, 128), F32),
            pltpu.VMEM((zn, FINE, 128), F32),
            dma((8,)),
            dma((chips,)),
            dma((2,)),
            dma((5,)),
            dma((5, side)),
            dma((5, side, side)),
            dma((5,)),
            dma((pieces, 2)),
            dma((pieces, 2, levels)),
            dma((pieces, 2, levels)),
            dma((2,)),
        ],
        compiler_params=pltpu.CompilerParams(
            collective_id=0, has_side_effects=True, vmem_limit_bytes=63 * 1024 * 1024
        ),
    )(in_one, in_two, l_one, l_two, l_pair, z_anc, linv_one, linv_two))


def solution(mesh):
    side = 1
    while side * side < mesh.shape["col"]:
        side += 1
    placed = (
        P("row", "col"),
        P(),
        P(),
        P(("row", "col"), None),
        P(("row", "col"), None),
        P("row", None),
        P(),
        P(),
    )
    return jax.shard_map(
        functools.partial(shards, side),
        mesh=mesh,
        in_specs=placed,
        out_specs=(
            P(("row", "col"), None),
            P("row", "col"),
            P(("row", "col"), None),
            P("row", "col"),
            P("row", "col"),
        ),
        check_vma=False,
    )
```

time: 112 us -> 92.7 us (0.83)
  Pallas kernels: 101 us -> 86.7 us
  local copies, waits for them, and re-layouts: 10.1 us -> 4 us
    pallas_call x1, Pallas kernels: 101 us -> 86.7 us  [shards(): pl.pallas_call(functools.partial(kernel, side, pieces), out_shape=(out(FI...]
    unnamed x21 -> x13, local copies, waits for them, and re-layouts: 10.1 us -> 4 us
where the time goes in v2:
time: 92.7 us; the launch traced here: 91.3 us
  Pallas kernels  86.7 us (94%)
  local copies, waits for them, and re-layouts  4 us (4%)
    pallas_call x1, Pallas kernels, shards(): pl.pallas_call(functools.partial(kernel, side, pieces), out_shape=(out(FI...  86.7 us
    unnamed x13, local copies, waits for them, and re-layouts  4 us

profile of v2, /device:TPU:1, one launch (start us, length us, event | category | flops | bytes accessed | tf_op | source)
XLA Modules:
  0.0 91.3 jit_solution(9191796473153350472)
XLA Ops:
  0.6 86.7 %shard_map.119 = (f32[16,512]{1,0:T(8,128)}, f32[16,32]{1,0:T(8,128)}, f32[16,512]{1,0:T(8,128)}, f32[16,32]{1,0:T(8,128)}, f32[16,32]{1,0:T(8,128)}) custom-call(s32[64]{0:T(128)} %in_one_hbm.1, s32[64]{0:T(128)} %in_two_hbm.1, f32[16,512]{1,0:T(8,128)} %l_one_hbm.1, f32[16,512]{1,0:T(8,128)} %l_two_hbm.1, f32[16,512]{1,0:T(8,128)} %l_pair_hbm.1, ...), custom_call_target="tpu_custom_call" | custom-call | tf_op jit(solution)/shard_map/pallas_call | solution.py:361
  87.3 0.0 copy-start.3
  87.3 0.0 copy-start
  87.3 1.4 %copy.18 = f32[16,512]{1,0:T(8,128)} copy(f32[16,512]{1,0:T(8,128)} %get-tuple-element.10) | data formatting | bytes 65536
  88.7 0.0 copy-done.3
  88.7 0.6 copy.19
  89.3 0.0 copy-done
  89.3 0.0 copy-start.2
  89.3 0.6 copy.20
  90.0 0.1 copy-done.2
  90.0 0.0 copy-start.1
  90.0 0.6 copy.21
  90.6 0.1 copy-done.1
  90.7 0.6 copy.22
Async XLA Ops:
  87.3 1.4 %copy-start.3 = (f32[16,32]{1,0:T(8,128)S(1)}, f32[16,32]{1,0:T(8,128)}, u32[]{:S(2)}) copy-start(f32[16,32]{1,0:T(8,128)} %get-tuple-element.11) | copy-start | bytes 6148
  87.3 2.0 %copy-start = (f32[16,512]{1,0:T(8,128)S(1)}, f32[16,512]{1,0:T(8,128)}, u32[]{:S(2)}) copy-start(f32[16,512]{1,0:T(8,128)} %get-tuple-element.12) | copy-start | bytes 98308
  89.3 0.7 copy-start.2
  90.0 0.7 copy-start.1

commit v3 on v2

--- a/solution.py
+++ b/solution.py
@@ -8,6 +8,8 @@
 from jax.sharding import PartitionSpec as P
 
 BLK = 128
+TREE = {8: 6, 7: 6, 6: 4, 5: 4, 4: 2, 3: 2, 2: 0, 1: 0}
+ORDER = ((8, 7), (6, 5), (4, 3), (2, 1))
 FINE = 16
 MESH = pl.DeviceIdType.MESH
 F32 = jnp.float32
@@ -38,10 +40,10 @@
 def kernel(
     side, pieces,
     in_one_hbm, in_two_hbm, l_one_hbm, l_two_hbm, l_pair_hbm, z_hbm, linv_one_hbm, linv_two_hbm,
-    col_one, diag_one, col_two, pair_block, diag_two,
+    cols_hbm, tiles_hbm,
     in_one, in_two, l_one, l_two, l_pair, z_v, linv_one, linv_two,
-    own, hop, far, near, res, m_high, m_low, part, even, odd, pack, got,
-    local_sem, hop_recv, far_recv, send_sem, first_recv, second_recv, core_recv, tree_send, even_recv, odd_recv, got_sem,
+    own, hop, far, near, corner, res, m_high, m_low, part, tree, pack, got, cols_v, tiles_v,
+    local_sem, hop_recv, far_recv, send_sem, first_recv, second_recv, core_recv, tree_send, tree_recv, got_sem,
 ):
     chips = side * side
     zn = chips
@@ -94,7 +96,7 @@
     mine_two = l_two[...] * flag_two
     near[here, :, :width] = mine_one
     near[here, :, width:2 * width] = mine_two
-    near[here, :, 2 * width:] = l_pair[...]
+    corner[here] = l_pair[...]
     tiles = width // 128
     for tile in range(2 * tiles):
         source = mine_one if tile < tiles else mine_two
@@ -104,27 +106,7 @@
 
     group = zn // 2
     lead = zn // 4
-    staged[5].wait()
-    turn = lax.rem(lead * FINE + (zn - col) * FINE, zn * FINE)
     depth = zn * FINE
-    z_parts = split(jnp.concatenate(
-        [pltpu.roll(z_v[:, n * depth:(n + 1) * depth], turn, 1) for n in range(2)], axis=1
-    ))
-
-    pl.semaphore_wait(barrier, chips + zn - 1)
-
-    mine = pltpu.make_async_copy(own.at[chip], hop.at[chip], hop_recv.at[chip])
-    mine.start()
-    for step in range(1, chips):
-        to = lax.rem(chip + step, chips)
-        send(own.at[to], hop.at[chip], send_sem.at[0], hop_recv.at[chip], (2 * to + core, col))
-    for step in sorted(range(1, zn), key=lambda n: -min(n, zn - n)):
-        to = lax.rem(col + step, zn)
-        spot = (lead - step) % zn
-        arrived(hop.at[to], hop_recv.at[to])
-        send(hop.at[to], far.at[here, spot], send_sem.at[1], far_recv.at[spot // group], (row, to))
-    arrived(hop.at[col], hop_recv.at[col])
-    far[here, lead] = hop[col]
 
     def place(first, second, which):
         xs = lax.rem(x + side + first * (1 - which) + second * which, side)
@@ -163,8 +145,34 @@
     def near_all(spot):
         return near.at[spot]
 
+    def corner_all(spot):
+        return corner.at[spot]
+
     def res_half(n):
         return lambda spot: res.at[n, spot]
+
+    pl.semaphore_wait(barrier, chips + zn - 1)
+
+    mine = pltpu.make_async_copy(own.at[chip], hop.at[chip], hop_recv.at[chip])
+    mine.start()
+    for step in range(1, chips):
+        to = lax.rem(chip + step, chips)
+        send(own.at[to], hop.at[chip], send_sem.at[0], hop_recv.at[chip], (2 * to + core, col))
+    spread_first(near_all, 3, 2)
+    spread_first(corner_all, 5, 5)
+    staged[5].wait()
+    turn = lax.rem(lead * FINE + (zn - col) * FINE, zn * FINE)
+    z_parts = split(jnp.concatenate(
+        [pltpu.roll(z_v[:, n * depth:(n + 1) * depth], turn, 1) for n in range(2)], axis=1
+    ))
+    for step in sorted(range(1, zn), key=lambda n: -min(n, zn - n)):
+        to = lax.rem(col + step, zn)
+        spot = (lead - step) % zn
+        arrived(hop.at[to], hop_recv.at[to])
+        send(hop.at[to], far.at[here, spot], send_sem.at[1], far_recv.at[spot // group], (row, to))
+    arrived(hop.at[col], hop_recv.at[col])
+    far[here, lead] = hop[col]
+    spread_second(near_all, 3, 2)
 
     arrived(far.at[0, pl.ds(0, group - 1)], far_recv.at[0])
     spread_first(far_half(0), 2, 0)
@@ -172,11 +180,12 @@
     spread_first(far_half(1), 2, 1)
     spread_second(far_half(0), 2, 0)
     spread_second(far_half(1), 2, 1)
+    spread_third(near_all, 3, 2)
     spread_third(far_half(0), 2, 0)
     spread_third(far_half(1), 2, 1)
     spread_end(far_half(0), 0)
+    spread_second(corner_all, 5, 5)
     spread_end(far_half(1), 1)
-    spread_first(near_all, 3, 2)
 
     for which in range(2):
         for tile in range(2 * tiles):
@@ -189,6 +198,7 @@
 
     most = zn // 2
     ways = (0, 1)
+    above = {d: TREE.get(d, 0) for d in range(1, most + 1)}
 
     def reach(piece, way):
         return most if (piece + way) % 2 == 0 else most - 1
@@ -196,75 +206,59 @@
     def along(way, distance):
         return lax.rem(col + (distance if way == 0 else zn - distance), zn)
 
-    def leaf(piece, way, distance):
-        if distance > reach(piece, way):
+    def gathered(piece, way, distance):
+        total = part[piece, along(way, distance)] if distance else None
+        for d in range(reach(piece, way), 0, -1):
+            if above[d] == distance:
+                arrived(tree.at[piece, way, d - 1], tree_recv.at[piece, way, d - 1])
+                value = tree[piece, way, d - 1]
+                total = value if total is None else total + value
+        return total
+
+    def pass_on(piece, way, distance):
+        last = reach(piece, way)
+        if distance > last:
             return
-        source = part.at[piece, along(way, distance)]
-        level = (distance - 1) // 2
-        if distance % 2:
-            send(source, odd.at[piece, way, level], tree_send.at[piece, way], odd_recv.at[piece, way, level],
-                 (row, along(way, 1)))
+        below = [d for d in range(1, last + 1) if above[d] == distance]
+        if below:
+            tree[piece, way, below[0] - 1] = gathered(piece, way, distance)
+            source = tree.at[piece, way, below[0] - 1]
         else:
-            send(source, even.at[piece, way, level], tree_send.at[piece, way], even_recv.at[piece, way, level],
-                 (row, along(way, 2)))
-
-    def gathered(piece, way, distance):
-        level = distance // 2
-        arrived(odd.at[piece, way, level], odd_recv.at[piece, way, level])
-        total = odd[piece, way, level]
-        if distance + 2 <= reach(piece, way):
-            arrived(even.at[piece, way, level], even_recv.at[piece, way, level])
-            total = total + even[piece, way, level]
-        return total
-
-    def chain(piece, way, distance):
-        if distance + 1 > reach(piece, way):
-            leaf(piece, way, distance)
-            return
-        level = distance // 2
-        odd[piece, way, level] = part[piece, along(way, distance)] + gathered(piece, way, distance)
-        send(odd.at[piece, way, level], even.at[piece, way, level - 1], tree_send.at[piece, way],
-             even_recv.at[piece, way, level - 1], (row, along(way, 2)))
+            source = part.at[piece, along(way, distance)]
+        send(source, tree.at[piece, way, distance - 1], tree_send.at[piece, way], tree_recv.at[piece, way, distance - 1],
+             (row, along(way, distance - above[distance])))
 
     share = 2 * width // pieces
+    turns = [[d for d in group if d <= most] for group in ORDER]
+    turns = [group for group in turns if group]
     for piece in range(pieces):
         cols = slice(piece * share, (piece + 1) * share)
         product = dot_parts(z_parts, (m_high[:, cols], m_low[:, cols]), ((1,), (0,)))
         part[piece] = product.reshape(zn, FINE, share)
         for way in ways:
-            leaf(piece, way, most)
-            leaf(piece, way, most - 1)
-    if most > 3:
+            for distance in turns[0]:
+                pass_on(piece, way, distance)
+    for n, group in enumerate(turns[1:]):
         for piece in range(pieces):
             for way in ways:
-                leaf(piece, way, most - 3)
-
-    for distance in range(most - 2, 0, -2):
-        for piece in range(pieces):
-            for way in ways:
-                chain(piece, way, distance)
-        if distance > 3:
-            for piece in range(pieces):
-                for way in ways:
-                    leaf(piece, way, distance - 3)
-        if distance == most - 2:
-            spread_second(near_all, 3, 2)
-        if distance == max(most - 4, 2):
-            spread_third(near_all, 3, 2)
-    if most <= 2:
-        spread_second(near_all, 3, 2)
-        spread_third(near_all, 3, 2)
+                for distance in group:
+                    pass_on(piece, way, distance)
+        if n == 1:
+            spread_third(corner_all, 5, 5)
+    if len(turns) < 3:
+        spread_third(corner_all, 5, 5)
 
     for copy in staged[6:]:
         copy.wait()
     inv_one = split(linv_one[...])
     inv_two = split(linv_two[...])
     spread_end(near_all, 2)
+    spread_end(corner_all, 5)
     count = 2 * chips * FINE
     near_one = split(near[:, :, :width].reshape(count, width))
     near_two = split(near[:, :, width:2 * width].reshape(count, width))
     pair = jnp.concatenate(
-        [near[which * chips + t, :, 2 * width:] for t in range(chips) for which in range(2)], axis=0
+        [corner[which * chips + t] for t in range(chips) for which in range(2)], axis=0
     )
     pair = split(pair)
     line = lax.broadcasted_iota(jnp.int32, (48, width), 0)
@@ -291,11 +285,13 @@
 
     y_one = nn(res[0, here], inv_one)
     one = -(flag_one * y_one)
-    col_one[...] = one
+    cols_v[0] = one
     spread_second(res_half(0), 4, 3)
     spread_second(res_half(1), 4, 4)
     y_two = nn(res[1, here] + nn(one, pair), inv_two)
-    col_two[...] = -(flag_two * y_two)
+    cols_v[1] = -(flag_two * y_two)
+    written = pltpu.make_async_copy(cols_v, cols_hbm, local_sem.at[0])
+    written.start()
     spread_third(res_half(0), 4, 3)
     spread_third(res_half(1), 4, 4)
     spread_end(res_half(0), 3)
@@ -329,20 +325,43 @@
     total = pack[col]
     for step in range(1, zn):
         total = total + got[step]
-    diag_one[...] = total[:, :32] + gram_one
-    pair_block[...] = -(pltpu.roll(total, 96, 1)[:, :32] + gram_pair)
-    diag_two[...] = pltpu.roll(total, 64, 1)[:, :32] + gram_two
+    grams = jnp.concatenate([gram_one, gram_pair, gram_two, jnp.zeros((FINE, 32), F32)], axis=1)
+    total = total + grams
+    tiles_v[...] = jnp.where((lanes >= 32) & (lanes < 64), -total, total)
+    ended = pltpu.make_async_copy(tiles_v, tiles_hbm, local_sem.at[1])
+    ended.start()
 
     arrived(own.at[pl.ds(0, chips - 1)], send_sem.at[0])
     arrived(hop.at[pl.ds(0, zn - 1)], send_sem.at[1])
     arrived(far.at[pl.ds(0, 2 * chips - 1)], send_sem.at[2])
     arrived(near.at[pl.ds(0, 2 * chips - 1)], send_sem.at[3])
+    arrived(corner.at[pl.ds(0, 2 * chips - 1)], send_sem.at[5])
     for n in range(2):
         arrived(res.at[n, pl.ds(0, 2 * chips - 1)], send_sem.at[4])
     for piece in range(pieces):
         for way in ways:
             arrived(part.at[piece, pl.ds(0, reach(piece, way))], tree_send.at[piece, way])
     arrived(got.at[pl.ds(1, zn - 1)], got_sem.at[0])
+    written.wait()
+    ended.wait()
+
+
+def deal(cols, tiles, col_one, diag_one, col_two, pair_block, diag_two, cols_v, tiles_v, out_v, sem):
+    loads = [pltpu.make_async_copy(cols, cols_v, sem.at[0]), pltpu.make_async_copy(tiles, tiles_v, sem.at[1])]
+    for copy in loads:
+        copy.start()
+    loads[1].wait()
+    stores = []
+    for n, target in enumerate((diag_one, pair_block, diag_two)):
+        out_v[n] = tiles_v[:, 32 * n:32 * n + 32]
+        stores.append(pltpu.make_async_copy(out_v.at[n], target, sem.at[2 + n]))
+        stores[-1].start()
+    loads[0].wait()
+    for n, target in enumerate((col_one, col_two)):
+        stores.append(pltpu.make_async_copy(cols_v.at[n], target, sem.at[5 + n]))
+        stores[-1].start()
+    for copy in stores:
+        copy.wait()
 
 
 def shards(side, z_anc, in_one, in_two, l_one, l_two, l_pair, linv_one, linv_two):
@@ -352,19 +371,15 @@
     rows, depth = z_anc.shape
     pieces = 4 if width > 128 else 2
     share = 2 * width // pieces
-    levels = zn // 4
-    vmem = pl.BlockSpec(memory_space=pltpu.VMEM)
     hbm = pl.BlockSpec(memory_space=pl.ANY)
     dma = pltpu.SemaphoreType.DMA
     out = lambda *shape: jax.ShapeDtypeStruct(shape, F32)
     held = lambda array: pltpu.VMEM(array.shape, array.dtype)
-    return tuple(pl.pallas_call(
+    cols, tiles = pl.pallas_call(
         functools.partial(kernel, side, pieces),
-        out_shape=(
-            out(FINE, width), out(16, 32), out(FINE, width), out(16, 32), out(16, 32),
-        ),
+        out_shape=(out(2, FINE, width), out(FINE, 128)),
         in_specs=[hbm] * 8,
-        out_specs=[vmem] * 5,
+        out_specs=[hbm] * 2,
         scratch_shapes=[
             pltpu.SMEM(in_one.shape, in_one.dtype),
             pltpu.SMEM(in_two.shape, in_two.dtype),
@@ -372,31 +387,43 @@
             pltpu.VMEM((chips, 8, 128), F32),
             pltpu.VMEM((chips, 8, 128), F32),
             pltpu.VMEM((2 * chips, zn, 8, 128), F32),
-            pltpu.VMEM((2 * chips, FINE, 3 * width), F32),
+            pltpu.VMEM((2 * chips, FINE, 2 * width), F32),
+            pltpu.VMEM((2 * chips, FINE, width), F32),
             pltpu.VMEM((2, 2 * chips, FINE, width), F32),
             pltpu.VMEM((depth, 2 * width), BF16),
             pltpu.VMEM((depth, 2 * width), BF16),
             pltpu.VMEM((pieces, zn, FINE, share), F32),
-            pltpu.VMEM((pieces, 2, levels, FINE, share), F32),
-            pltpu.VMEM((pieces, 2, levels, FINE, share), F32),
+            pltpu.VMEM((pieces, 2, zn // 2, FINE, share), F32),
             pltpu.VMEM((zn, FINE, 128), F32),
             pltpu.VMEM((zn, FINE, 128), F32),
+            pltpu.VMEM((2, FINE, width), F32),
+            pltpu.VMEM((FINE, 128), F32),
             dma((8,)),
             dma((chips,)),
             dma((2,)),
-            dma((5,)),
-            dma((5, side)),
-            dma((5, side, side)),
-            dma((5,)),
+            dma((6,)),
+            dma((6, side)),
+            dma((6, side, side)),
+            dma((6,)),
             dma((pieces, 2)),
-            dma((pieces, 2, levels)),
-            dma((pieces, 2, levels)),
+            dma((pieces, 2, zn // 2)),
             dma((2,)),
         ],
         compiler_params=pltpu.CompilerParams(
             collective_id=0, has_side_effects=True, vmem_limit_bytes=63 * 1024 * 1024
         ),
-    )(in_one, in_two, l_one, l_two, l_pair, z_anc, linv_one, linv_two))
+    )(in_one, in_two, l_one, l_two, l_pair, z_anc, linv_one, linv_two)
+    return tuple(pl.pallas_call(
+        deal,
+        out_shape=(
+            out(FINE, width), out(16, 32), out(FINE, width), out(16, 32), out(16, 32),
+        ),
+        in_specs=[hbm] * 2,
+        out_specs=[hbm] * 5,
+        scratch_shapes=[
+            pltpu.VMEM((2, FINE, width), F32), pltpu.VMEM((FINE, 128), F32), pltpu.VMEM((3, 16, 32), F32), dma((7,)),
+        ],
+    )(cols, tiles))
 
 
 def solution(mesh):

time: 92.7 us -> 87.4 us (0.943); the launches traced: 91.3 us -> 87.2 us
  local copies, waits for them, and re-layouts: 4 us -> 0 us
    unnamed x13 -> x0, local copies, waits for them, and re-layouts: 4 us -> none
    pallas_call x1 -> x2, Pallas kernels: 86.7 us -> 86.5 us  [the longest x1 85 us: shards(): pl.pallas_call(functools.partial(kernel, side, pieces), out_shape=(out(2,...]
where the time goes in v3:
time: 87.4 us; the launch traced here: 87.2 us
  Pallas kernels  86.5 us (99%)
    pallas_call x1, Pallas kernels, shards(): pl.pallas_call(functools.partial(kernel, side, pieces), out_shape=(out(2,...  85 us

profile of v3, /device:TPU:1, one launch (start us, length us, event | category | flops | bytes accessed | tf_op | source)
XLA Modules:
  0.0 87.2 jit_solution(7597571653010104210)
XLA Ops:
  0.6 85.0 %shard_map.119 = (f32[2,16,512]{2,1,0:T(8,128)}, f32[16,128]{1,0:T(8,128)}) custom-call(s32[64]{0:T(128)} %in_one_hbm.1, s32[64]{0:T(128)} %in_two_hbm.1, f32[16,512]{1,0:T(8,128)} %l_one_hbm.1, f32[16,512]{1,0:T(8,128)} %l_two_hbm.1, f32[16,512]{1,0:T(8,128)} %l_pair_hbm.1, f32[256,512]{1,0:T(8,128)} %z_hbm.1, f32[512,512]{1,0:T(8,128)} %linv_one_hbm.1, ...), custom_call_target="tpu_custom_call" | custom-call | tf_op jit(solution)/shard_map/pallas_call | solution.py:378
  85.6 1.5 %shard_map.120 = (f32[16,512]{1,0:T(8,128)}, f32[16,32]{1,0:T(8,128)}, f32[16,512]{1,0:T(8,128)}, f32[16,32]{1,0:T(8,128)}, f32[16,32]{1,0:T(8,128)}) custom-call(f32[2,16,512]{2,1,0:T(8,128)} %get-tuple-element.7.cols, f32[16,128]{1,0:T(8,128)} %get-tuple-element.8.tiles), custom_call_target="tpu_custom_call" | custom-call | tf_op jit(solution)/shard_map/pallas_call | solution.py:416

commit v4 on v3

--- a/solution.py
+++ b/solution.py
@@ -42,7 +42,7 @@
     in_one_hbm, in_two_hbm, l_one_hbm, l_two_hbm, l_pair_hbm, z_hbm, linv_one_hbm, linv_two_hbm,
     cols_hbm, tiles_hbm,
     in_one, in_two, l_one, l_two, l_pair, z_v, linv_one, linv_two,
-    own, hop, far, near, corner, res, m_high, m_low, part, tree, pack, got, cols_v, tiles_v,
+    own, hop, far, near, corner, res, m_high, m_low, part, tree, pack, got, cols_v, tiles_v, told,
     local_sem, hop_recv, far_recv, send_sem, first_recv, second_recv, core_recv, tree_send, tree_recv, got_sem,
 ):
     chips = side * side
@@ -81,11 +81,22 @@
     def greet(device):
         pl.semaphore_signal(barrier, inc=1, device_id=device, device_id_type=MESH)
 
+    low = row - core
+    greet((sibling, col))
     for step in sorted(range(1, zn), key=lambda n: -min(n, zn - n)):
-        greet((row, lax.rem(col + step, zn)))
+        greet((low, lax.rem(col + step, zn)))
     for step in range(1, chips):
-        greet((2 * lax.rem(chip + step, chips) + core, col))
-    greet((sibling, col))
+        greet((2 * lax.rem(chip + step, chips) + 1, col))
+
+    def hear(heard, own_part):
+        @pl.when(core == own_part)
+        def _():
+            pl.semaphore_wait(barrier, heard)
+            pl.semaphore_signal(told, inc=1, device_id=(sibling, col), device_id_type=MESH)
+
+        @pl.when(core != own_part)
+        def _():
+            pl.semaphore_wait(told, 1)
 
     for copy in staged[:5]:
         copy.wait()
@@ -151,7 +162,7 @@
     def res_half(n):
         return lambda spot: res.at[n, spot]
 
-    pl.semaphore_wait(barrier, chips + zn - 1)
+    hear(2 * chips - 1, 1)
 
     mine = pltpu.make_async_copy(own.at[chip], hop.at[chip], hop_recv.at[chip])
     mine.start()
@@ -162,9 +173,10 @@
     spread_first(corner_all, 5, 5)
     staged[5].wait()
     turn = lax.rem(lead * FINE + (zn - col) * FINE, zn * FINE)
-    z_parts = split(jnp.concatenate(
-        [pltpu.roll(z_v[:, n * depth:(n + 1) * depth], turn, 1) for n in range(2)], axis=1
-    ))
+    z_parts = [
+        split(pltpu.roll(z_v[:, pl.ds(pl.multiple_of(which * depth, depth), depth)], turn, 1)) for which in (core, 1 - core)
+    ]
+    hear(2 * zn - 1, 0)
     for step in sorted(range(1, zn), key=lambda n: -min(n, zn - n)):
         to = lax.rem(col + step, zn)
         spot = (lead - step) % zn
@@ -183,18 +195,31 @@
     spread_third(near_all, 3, 2)
     spread_third(far_half(0), 2, 0)
     spread_third(far_half(1), 2, 1)
-    spread_end(far_half(0), 0)
     spread_second(corner_all, 5, 5)
-    spread_end(far_half(1), 1)
-
-    for which in range(2):
+
+    share = 2 * width // pieces
+
+    def product(n, which):
         for tile in range(2 * tiles):
             at = which * chips + 2 * tile
             value = jnp.stack([far[at], far[at + 1]], axis=1).reshape(depth, 128)
             high, low = split(value)
-            rows = slice(which * depth, (which + 1) * depth)
-            m_high[rows, tile * 128:tile * 128 + 128] = high
-            m_low[rows, tile * 128:tile * 128 + 128] = low
+            m_high[n, :, tile * 128:tile * 128 + 128] = high
+            m_low[n, :, tile * 128:tile * 128 + 128] = low
+
+        def of(piece):
+            cols = slice(piece * share, (piece + 1) * share)
+            value = dot_parts(z_parts[n], (m_high[n, :, cols], m_low[n, :, cols]), ((1,), (0,)))
+            return value.reshape(zn, FINE, share)
+
+        return of
+
+    ready = product(0, core)
+    for piece in range(pieces):
+        part[piece] = ready(piece)
+    spread_end(far_half(0), 0)
+    spread_end(far_half(1), 1)
+    ready = product(1, 1 - core)
 
     most = zn // 2
     ways = (0, 1)
@@ -228,13 +253,10 @@
         send(source, tree.at[piece, way, distance - 1], tree_send.at[piece, way], tree_recv.at[piece, way, distance - 1],
              (row, along(way, distance - above[distance])))
 
-    share = 2 * width // pieces
     turns = [[d for d in group if d <= most] for group in ORDER]
     turns = [group for group in turns if group]
     for piece in range(pieces):
-        cols = slice(piece * share, (piece + 1) * share)
-        product = dot_parts(z_parts, (m_high[:, cols], m_low[:, cols]), ((1,), (0,)))
-        part[piece] = product.reshape(zn, FINE, share)
+        part[piece] = part[piece] + ready(piece)
         for way in ways:
             for distance in turns[0]:
                 pass_on(piece, way, distance)
@@ -390,14 +412,15 @@
             pltpu.VMEM((2 * chips, FINE, 2 * width), F32),
             pltpu.VMEM((2 * chips, FINE, width), F32),
             pltpu.VMEM((2, 2 * chips, FINE, width), F32),
-            pltpu.VMEM((depth, 2 * width), BF16),
-            pltpu.VMEM((depth, 2 * width), BF16),
+            pltpu.VMEM((2, depth // 2, 2 * width), BF16),
+            pltpu.VMEM((2, depth // 2, 2 * width), BF16),
             pltpu.VMEM((pieces, zn, FINE, share), F32),
             pltpu.VMEM((pieces, 2, zn // 2, FINE, share), F32),
             pltpu.VMEM((zn, FINE, 128), F32),
             pltpu.VMEM((zn, FINE, 128), F32),
             pltpu.VMEM((2, FINE, width), F32),
             pltpu.VMEM((FINE, 128), F32),
+            pltpu.SemaphoreType.REGULAR,
             dma((8,)),
             dma((chips,)),
             dma((2,)),

time: 87.4 us -> 85.5 us (0.978)
  Pallas kernels: 86.5 us -> 84.7 us
    pallas_call x1, Pallas kernels: 85 us -> 83.2 us  [shards(): pl.pallas_call(functools.partial(kernel, side, pieces), out_shape=(out(2,...]
where the time goes in v4:
time: 85.5 us; the launch traced here: 85.3 us
  Pallas kernels  84.7 us (99%)
    pallas_call x1, Pallas kernels, shards(): pl.pallas_call(functools.partial(kernel, side, pieces), out_shape=(out(2,...  83.2 us

profile of v4, /device:TPU:1, one launch (start us, length us, event | category | flops | bytes accessed | tf_op | source)
XLA Modules:
  0.0 85.3 jit_solution(17793920274266688920)
XLA Ops:
  0.6 83.2 %shard_map.119 = (f32[2,16,512]{2,1,0:T(8,128)}, f32[16,128]{1,0:T(8,128)}) custom-call(s32[64]{0:T(128)} %in_one_hbm.1, s32[64]{0:T(128)} %in_two_hbm.1, f32[16,512]{1,0:T(8,128)} %l_one_hbm.1, f32[16,512]{1,0:T(8,128)} %l_two_hbm.1, f32[16,512]{1,0:T(8,128)} %l_pair_hbm.1, f32[256,512]{1,0:T(8,128)} %z_hbm.1, f32[512,512]{1,0:T(8,128)} %linv_one_hbm.1, ...), custom_call_target="tpu_custom_call" | custom-call | tf_op jit(solution)/shard_map/pallas_call | solution.py:400
  83.8 1.5 %shard_map.120 = (f32[16,512]{1,0:T(8,128)}, f32[16,32]{1,0:T(8,128)}, f32[16,512]{1,0:T(8,128)}, f32[16,32]{1,0:T(8,128)}, f32[16,32]{1,0:T(8,128)}) custom-call(f32[2,16,512]{2,1,0:T(8,128)} %get-tuple-element.7.cols, f32[16,128]{1,0:T(8,128)} %get-tuple-element.8.tiles), custom_call_target="tpu_custom_call" | custom-call | tf_op jit(solution)/shard_map/pallas_call | solution.py:439

commit v5 on v4

--- a/solution.py
+++ b/solution.py
@@ -40,9 +40,9 @@
 def kernel(
     side, pieces,
     in_one_hbm, in_two_hbm, l_one_hbm, l_two_hbm, l_pair_hbm, z_hbm, linv_one_hbm, linv_two_hbm,
-    cols_hbm, tiles_hbm,
+    cols_v, tiles_v,
     in_one, in_two, l_one, l_two, l_pair, z_v, linv_one, linv_two,
-    own, hop, far, near, corner, res, m_high, m_low, part, tree, pack, got, cols_v, tiles_v, told,
+    own, hop, far, near, corner, res, m_high, m_low, part, tree, pack, got, told,
     local_sem, hop_recv, far_recv, send_sem, first_recv, second_recv, core_recv, tree_send, tree_recv, got_sem,
 ):
     chips = side * side
@@ -169,8 +169,6 @@
     for step in range(1, chips):
         to = lax.rem(chip + step, chips)
         send(own.at[to], hop.at[chip], send_sem.at[0], hop_recv.at[chip], (2 * to + core, col))
-    spread_first(near_all, 3, 2)
-    spread_first(corner_all, 5, 5)
     staged[5].wait()
     turn = lax.rem(lead * FINE + (zn - col) * FINE, zn * FINE)
     z_parts = [
@@ -184,7 +182,8 @@
         send(hop.at[to], far.at[here, spot], send_sem.at[1], far_recv.at[spot // group], (row, to))
     arrived(hop.at[col], hop_recv.at[col])
     far[here, lead] = hop[col]
-    spread_second(near_all, 3, 2)
+    spread_first(near_all, 3, 2)
+    spread_first(corner_all, 5, 5)
 
     arrived(far.at[0, pl.ds(0, group - 1)], far_recv.at[0])
     spread_first(far_half(0), 2, 0)
@@ -192,9 +191,9 @@
     spread_first(far_half(1), 2, 1)
     spread_second(far_half(0), 2, 0)
     spread_second(far_half(1), 2, 1)
-    spread_third(near_all, 3, 2)
     spread_third(far_half(0), 2, 0)
     spread_third(far_half(1), 2, 1)
+    spread_second(near_all, 3, 2)
     spread_second(corner_all, 5, 5)
 
     share = 2 * width // pieces
@@ -266,8 +265,10 @@
                 for distance in group:
                     pass_on(piece, way, distance)
         if n == 1:
+            spread_third(near_all, 3, 2)
             spread_third(corner_all, 5, 5)
     if len(turns) < 3:
+        spread_third(near_all, 3, 2)
         spread_third(corner_all, 5, 5)
 
     for copy in staged[6:]:
@@ -312,8 +313,6 @@
     spread_second(res_half(1), 4, 4)
     y_two = nn(res[1, here] + nn(one, pair), inv_two)
     cols_v[1] = -(flag_two * y_two)
-    written = pltpu.make_async_copy(cols_v, cols_hbm, local_sem.at[0])
-    written.start()
     spread_third(res_half(0), 4, 3)
     spread_third(res_half(1), 4, 4)
     spread_end(res_half(0), 3)
@@ -350,8 +349,6 @@
     grams = jnp.concatenate([gram_one, gram_pair, gram_two, jnp.zeros((FINE, 32), F32)], axis=1)
     total = total + grams
     tiles_v[...] = jnp.where((lanes >= 32) & (lanes < 64), -total, total)
-    ended = pltpu.make_async_copy(tiles_v, tiles_hbm, local_sem.at[1])
-    ended.start()
 
     arrived(own.at[pl.ds(0, chips - 1)], send_sem.at[0])
     arrived(hop.at[pl.ds(0, zn - 1)], send_sem.at[1])
@@ -364,23 +361,16 @@
         for way in ways:
             arrived(part.at[piece, pl.ds(0, reach(piece, way))], tree_send.at[piece, way])
     arrived(got.at[pl.ds(1, zn - 1)], got_sem.at[0])
-    written.wait()
-    ended.wait()
-
-
-def deal(cols, tiles, col_one, diag_one, col_two, pair_block, diag_two, cols_v, tiles_v, out_v, sem):
-    loads = [pltpu.make_async_copy(cols, cols_v, sem.at[0]), pltpu.make_async_copy(tiles, tiles_v, sem.at[1])]
-    for copy in loads:
-        copy.start()
-    loads[1].wait()
+
+
+def deal(cols, tiles, col_one, diag_one, col_two, pair_block, diag_two, out_v, sem):
     stores = []
+    for n, target in enumerate((col_one, col_two)):
+        stores.append(pltpu.make_async_copy(cols.at[n], target, sem.at[n]))
+        stores[-1].start()
     for n, target in enumerate((diag_one, pair_block, diag_two)):
-        out_v[n] = tiles_v[:, 32 * n:32 * n + 32]
+        out_v[n] = tiles[:, 32 * n:32 * n + 32]
         stores.append(pltpu.make_async_copy(out_v.at[n], target, sem.at[2 + n]))
-        stores[-1].start()
-    loads[0].wait()
-    for n, target in enumerate((col_one, col_two)):
-        stores.append(pltpu.make_async_copy(cols_v.at[n], target, sem.at[5 + n]))
         stores[-1].start()
     for copy in stores:
         copy.wait()
@@ -394,14 +384,15 @@
     pieces = 4 if width > 128 else 2
     share = 2 * width // pieces
     hbm = pl.BlockSpec(memory_space=pl.ANY)
+    vmem = pl.BlockSpec(memory_space=pltpu.VMEM)
     dma = pltpu.SemaphoreType.DMA
     out = lambda *shape: jax.ShapeDtypeStruct(shape, F32)
     held = lambda array: pltpu.VMEM(array.shape, array.dtype)
     cols, tiles = pl.pallas_call(
         functools.partial(kernel, side, pieces),
-        out_shape=(out(2, FINE, width), out(FINE, 128)),
-        in_specs=[hbm] * 8,
-        out_specs=[hbm] * 2,
+        out_shape=(pltpu.VMEM((2, FINE, width), F32), pltpu.VMEM((FINE, 128), F32)),
+        in_specs=[pl.BlockSpec(memory_space=pltpu.HBM)] * 8,
+        out_specs=[vmem] * 2,
         scratch_shapes=[
             pltpu.SMEM(in_one.shape, in_one.dtype),
             pltpu.SMEM(in_two.shape, in_two.dtype),
@@ -418,8 +409,6 @@
             pltpu.VMEM((pieces, 2, zn // 2, FINE, share), F32),
             pltpu.VMEM((zn, FINE, 128), F32),
             pltpu.VMEM((zn, FINE, 128), F32),
-            pltpu.VMEM((2, FINE, width), F32),
-            pltpu.VMEM((FINE, 128), F32),
             pltpu.SemaphoreType.REGULAR,
             dma((8,)),
             dma((chips,)),
@@ -441,11 +430,10 @@
         out_shape=(
             out(FINE, width), out(16, 32), out(FINE, width), out(16, 32), out(16, 32),
         ),
-        in_specs=[hbm] * 2,
+        in_specs=[vmem] * 2,
         out_specs=[hbm] * 5,
-        scratch_shapes=[
-            pltpu.VMEM((2, FINE, width), F32), pltpu.VMEM((FINE, 128), F32), pltpu.VMEM((3, 16, 32), F32), dma((7,)),
-        ],
+        scratch_shapes=[pltpu.VMEM((3, 16, 32), F32), dma((5,))],
+        compiler_params=pltpu.CompilerParams(vmem_limit_bytes=4 * 1024 * 1024),
     )(cols, tiles))
 
 

time: 85.5 us -> 84.2 us (0.985)
  Pallas kernels: 84.7 us -> 83.4 us
where the time goes in v5:
time: 84.2 us; the launch traced here: 84.1 us
  Pallas kernels  83.4 us (99%)
    pallas_call x1, Pallas kernels, shards(): pl.pallas_call(functools.partial(kernel, side, pieces), out_shape=(pltpu....  82.7 us

profile of v5, /device:TPU:1, one launch (start us, length us, event | category | flops | bytes accessed | tf_op | source)
XLA Modules:
  0.0 84.1 jit_solution(6473743268473297994)
XLA Ops:
  0.6 82.7 %shard_map.119 = (f32[2,16,512]{2,1,0:T(8,128)S(1)}, f32[16,128]{1,0:T(8,128)S(1)}) custom-call(s32[64]{0:T(128)} %in_one_hbm.1, s32[64]{0:T(128)} %in_two_hbm.1, f32[16,512]{1,0:T(8,128)} %l_one_hbm.1, f32[16,512]{1,0:T(8,128)} %l_two_hbm.1, f32[16,512]{1,0:T(8,128)} %l_pair_hbm.1, f32[256,512]{1,0:T(8,128)} %z_hbm.1, f32[512,512]{1,0:T(8,128)} %linv_one_hbm.1, ...), custom_call_target="tpu_custom_call" | custom-call | tf_op jit(solution)/shard_map/pallas_call | solution.py:391
  83.3 0.7 shard_map.120

commit v6 on v5

--- a/solution.py
+++ b/solution.py
@@ -338,7 +338,8 @@
             if shift:
                 piece = pltpu.roll(piece, shift, 1)
             packed = jnp.where((lanes >= 32 * n) & (lanes < 32 * n + 32), piece, packed)
-        pack[owner] = packed
+        rest = jnp.concatenate([pltpu.roll(packed[12:], 96 - 32 * n, 1) for n in range(3)], axis=0)
+        pack[owner] = jnp.where(lanes[:12] >= 96, rest, packed[:12])
     for step in sorted(range(1, zn), key=lambda n: -min(n, zn - n)):
         to = lax.rem(col + step, zn)
         send(pack.at[to], got.at[step], got_sem.at[0], got_sem.at[1], (row, to))
@@ -347,7 +348,11 @@
     for step in range(1, zn):
         total = total + got[step]
     grams = jnp.concatenate([gram_one, gram_pair, gram_two, jnp.zeros((FINE, 32), F32)], axis=1)
-    total = total + grams
+    rest = jnp.zeros((4, 128), F32)
+    for n in range(3):
+        piece = pltpu.roll(total[4 * n:4 * n + 4], 32 + 32 * n, 1)
+        rest = jnp.where((lanes[:4] >= 32 * n) & (lanes[:4] < 32 * n + 32), piece, rest)
+    total = jnp.concatenate([total, rest], axis=0) + grams
     tiles_v[...] = jnp.where((lanes >= 32) & (lanes < 64), -total, total)
 
     arrived(own.at[pl.ds(0, chips - 1)], send_sem.at[0])
@@ -407,8 +412,8 @@
             pltpu.VMEM((2, depth // 2, 2 * width), BF16),
             pltpu.VMEM((pieces, zn, FINE, share), F32),
             pltpu.VMEM((pieces, 2, zn // 2, FINE, share), F32),
-            pltpu.VMEM((zn, FINE, 128), F32),
-            pltpu.VMEM((zn, FINE, 128), F32),
+            pltpu.VMEM((zn, 12, 128), F32),
+            pltpu.VMEM((zn, 12, 128), F32),
             pltpu.SemaphoreType.REGULAR,
             dma((8,)),
             dma((chips,)),

time: 84.2 us -> 82.3 us (0.977)
  Pallas kernels: 83.4 us -> 81.2 us
    pallas_call x1, Pallas kernels: 82.7 us -> 80.5 us  [shards(): pl.pallas_call(functools.partial(kernel, side, pieces), out_shape=(pltpu....]
where the time goes in v6:
time: 82.3 us; the launch traced here: 81.9 us
  Pallas kernels  81.2 us (99%)
    pallas_call x1, Pallas kernels, shards(): pl.pallas_call(functools.partial(kernel, side, pieces), out_shape=(pltpu....  80.5 us

profile of v6, /device:TPU:1, one launch (start us, length us, event | category | flops | bytes accessed | tf_op | source)
XLA Modules:
  0.0 81.9 jit_solution(14492321231728214783)
XLA Ops:
  0.6 80.5 %shard_map.119 = (f32[2,16,512]{2,1,0:T(8,128)S(1)}, f32[16,128]{1,0:T(8,128)S(1)}) custom-call(s32[64]{0:T(128)} %in_one_hbm.1, s32[64]{0:T(128)} %in_two_hbm.1, f32[16,512]{1,0:T(8,128)} %l_one_hbm.1, f32[16,512]{1,0:T(8,128)} %l_two_hbm.1, f32[16,512]{1,0:T(8,128)} %l_pair_hbm.1, f32[256,512]{1,0:T(8,128)} %z_hbm.1, f32[512,512]{1,0:T(8,128)} %linv_one_hbm.1, ...), custom_call_target="tpu_custom_call" | custom-call | tf_op jit(solution)/shard_map/pallas_call | solution.py:396
  81.2 0.7 shard_map.120
